TPU v7x, 512 devices: a whole 4x4x16 slice. The times are simulated.
512 devices in a mesh: cells: 64 (over x, z), genes: 8 (over y, core).
Axes of the slice: x: 4, y: 4, z: 16, core: 2. Of those that a mesh axis runs over, the one named last changes fastest.
Arguments:
- expression: bfloat16 [262144, 4096], P('cells', 'genes'), may hold values from 0 to 3
- loading: bfloat16 [4096, 128], P('genes'), may hold values from -0.09375 to 0.09375
- kernel_width: bfloat16 [262144], P(('cells', 'genes')), may hold values from 10 to 20
- cluster: int32 [262144, 1], P(('cells', 'genes')), may hold values from 0 to 511, as said below
- quality: int32 [262144], P(('cells', 'genes')), may hold values from 0 to 1, as said below
Outputs:
- smoothed: float32 [262144, 128], P(('cells', 'genes'))
Inputs may be any that keep to these rules, and one draw needn't show every extreme that they name: Among the 512 cells of one device no cluster appears more than 2 times; one cluster appears exactly 2 times in every device, so that it holds 1024 cells; every cluster appears somewhere. All cells of a cluster that holds 1024 cells have quality 1.
All inputs are finite; a program needn't handle non-finite values.
Results may differ from a plain program's by a relative error of at most 0.0029.
Values may be sent and summed in bfloat16 or wider, within the bound.
A program may use at most 64 MiB of HBM per device.

v0:
```python
import jax
import jax.numpy as jnp
from jax import lax
from jax.sharding import PartitionSpec as P


def in_blocks(array, dim, size):
    dims = array.shape
    parts = array.reshape(*dims[:dim], size, dims[dim] // size, *dims[dim + 1 :])
    return jnp.moveaxis(parts, dim, 0)


def laid_out(parts, dim):
    parts = jnp.moveaxis(parts, 0, dim)
    dims = parts.shape
    return parts.reshape(*dims[:dim], dims[dim] * dims[dim + 1], *dims[dim + 2 :])


def exchange_both(array, axis, axes, splits, concats):
    sizes = [lax.axis_size(a) for a in axes]
    parts = in_blocks(array, splits[0], sizes[0])
    parts = jnp.moveaxis(in_blocks(parts, splits[1] + 1, sizes[1]), 0, 1)
    inside = parts.shape[2:]
    parts = parts.reshape(-1, *inside)
    parts = lax.all_to_all(parts, axis, split_axis=0, concat_axis=0, tiled=True)
    parts = laid_out(parts.reshape(*sizes, *inside), concats[0] + 1)
    return laid_out(parts, concats[1])


def diffuse(slot_rows, widths):
    widths = widths.astype(jnp.float32)
    present = (widths > 0).astype(jnp.float32)
    as_float = slot_rows.astype(jnp.float32)
    sq_norms = jnp.sum(as_float * as_float, axis=1)
    products = jnp.dot(slot_rows, slot_rows.T, preferred_element_type=jnp.float32)
    distance = sq_norms[:, None] + sq_norms[None, :] - 2.0 * products
    pair_live = present[:, None] * present[None, :]
    width_pair = jnp.where(
        pair_live > 0, widths[:, None] * widths[None, :], jnp.ones_like(pair_live)
    )
    affinity = jnp.exp(-distance / width_pair) * pair_live
    row_total = jnp.sum(affinity, axis=1) + (1.0 - present)
    weights = (affinity / row_total[:, None]).astype(jnp.bfloat16)
    one_step = 0.5 * (as_float + jnp.dot(weights, slot_rows, preferred_element_type=jnp.float32))
    two_steps = 0.5 * (
        one_step
        + jnp.dot(weights, one_step.astype(jnp.bfloat16), preferred_element_type=jnp.float32)
    )
    return two_steps


def body(expression, loading, kernel_width, cluster, quality):
    gene_count = lax.axis_size("genes")
    cell_count = lax.axis_size("cells")
    devices = gene_count * cell_count
    local_rows = kernel_width.shape[0]
    capacity = max(1, 2 * local_rows // devices)
    slot_count = devices * capacity
    comp_width = loading.shape[1]
    embedded = lax.psum_scatter(
        jnp.dot(expression, loading, preferred_element_type=jnp.float32),
        "genes",
        scatter_dimension=0,
        tiled=True,
    )
    embedded = embedded.astype(jnp.bfloat16)
    is_live = quality == 1
    destination = cluster[:, 0]
    owner_cell = destination // gene_count
    owner_gene = destination % gene_count
    positions = jnp.arange(local_rows, dtype=jnp.int32)
    same_dest = (
        (destination[:, None] == destination[None, :])
        & is_live[None, :]
        & (positions[None, :] < positions[:, None])
    )
    slot_rank = jnp.sum(same_dest.astype(jnp.int32), axis=1)
    slot_index = jnp.where(
        is_live, (owner_gene * cell_count + owner_cell) * capacity + slot_rank, -1
    )
    onehot = (jnp.arange(slot_count, dtype=jnp.int32)[:, None] == slot_index[None, :]).astype(
        jnp.bfloat16
    )
    packed = jnp.dot(onehot, embedded, preferred_element_type=jnp.float32).astype(jnp.bfloat16)
    packed = packed.reshape(gene_count, cell_count, capacity, comp_width)
    packed_band = jnp.dot(onehot, kernel_width, preferred_element_type=jnp.float32).astype(
        jnp.bfloat16
    )
    packed_band = packed_band.reshape(gene_count, cell_count, capacity)
    arrived, arrived_band = (
        exchange_both(packed, ("cells", "genes"), ("cells", "genes"), (1, 0), (1, 0)),
        exchange_both(packed_band, ("cells", "genes"), ("cells", "genes"), (1, 0), (1, 0)),
    )
    smoothed = diffuse(arrived.reshape(slot_count, comp_width), arrived_band.reshape(slot_count))
    returned = exchange_both(
        smoothed.reshape(gene_count, cell_count, capacity, comp_width),
        ("cells", "genes"),
        ("cells", "genes"),
        (1, 0),
        (1, 0),
    )
    picked = jnp.take(returned.reshape(slot_count, comp_width), jnp.maximum(slot_index, 0), axis=0)
    return jnp.where(is_live[:, None], picked, embedded.astype(jnp.float32))


def solution(mesh):
    return jax.shard_map(
        body,
        mesh=mesh,
        in_specs=(
            P("cells", "genes"),
            P("genes", None),
            P(("cells", "genes")),
            P(("cells", "genes"), None),
            P(("cells", "genes")),
        ),
        out_specs=P(("cells", "genes"), None),
        check_vma=False,
    )
```

profile of v0, /device:TPU:1, one launch (start us, length us, event | category | flops | bytes accessed | tf_op | source)
XLA Modules:
  0.0 166.1 jit_solution(6421638413152997109)
XLA Ops:
  6.5 0.0 copy-start
  6.5 0.0 copy-start.4
  6.5 0.0 copy-start.3
  6.5 0.0 copy-start.2
  6.5 0.0 reduce-scatter.2.cloned.1.call-start
  6.6 0.9 copy-done
  7.4 4.8 %fusion.19 = f32[4096,128]{1,0:T(8,128)} fusion(bf16[4096,512]{1,0:T(8,128)(2,1)} %param.5, bf16[512,128]{1,0:T(8,128)(2,1)S(1)} %copy-done), kind=kOutput, calls=%fused_computation.45 | convolution fusion | flops 536870912 | bytes 6422528 | tf_op jit(solution)/shard_map/dot_general | solution.py:61
  12.2 0.0 reduce-scatter.2.cloned.1.call-update
  12.2 0.0 copy-done.4
  12.3 0.0 copy-done.3
  12.3 0.0 copy-done.2
  12.3 0.3 convert_reduce_fusion
  12.6 0.5 fusion
  13.0 0.3 reshape_reshape.20
  13.3 0.5 copy.49
  13.8 0.1 reshape_reshape.21
  13.9 0.9 copy.50
  14.9 24.3 %all-to-all-start.1 = ((bf16[512,1,1,2]{3,2,1,0:T(2,128)(2,1)}), bf16[512,1,1,2]{3,2,1,0:T(2,128)(2,1)S(1)}, u32[]{:S(2)}, u32[]{:S(2)}) async-start(bf16[512,1,1,2]{3,2,1,0:T(2,128)(2,1)} %copy.50), calls=%async_computation.2 | async-start | bytes 524288 | tf_op jit(solution)/shard_map/all_to_all | solution.py:25
  39.2 18.8 %reduce-scatter.2.cloned.1.call-done = f32[512,128]{1,0:T(8,128)} async-done(((f32[4096,128]{1,0:T(8,128)}), f32[512,128]{1,0:T(8,128)}) %reduce-scatter.2.cloned.1.call-update) | async-done | bytes 262160 | tf_op jit(solution)/shard_map/reduce_scatter | solution.py:60
  58.0 1.4 fusion.4
  59.4 0.2 copy.66
  59.6 1.0 copy.45
  60.5 3.3 %all-to-all-done.1 = bf16[512,1,1,2]{3,2,1,0:T(2,128)(2,1)S(1)} async-done(((bf16[512,1,1,2]{3,2,1,0:T(2,128)(2,1)}), bf16[512,1,1,2]{3,2,1,0:T(2,128)(2,1)S(1)}, u32[]{:S(2)}, u32[]{:S(2)}) %all-to-all-start.1) | async-done | bytes 2080 | tf_op jit(solution)/shard_map/all_to_all | solution.py:25
  63.8 16.8 %all-to-all-start = ((bf16[512,1,1,2,128]{4,3,2,1,0:T(2,128)(2,1)}), bf16[512,1,1,2,128]{4,3,2,1,0:T(2,128)(2,1)S(1)}, u32[]{:S(2)}, u32[]{:S(2)}) async-start(bf16[512,1,1,2,128]{4,3,2,1,0:T(2,128)(2,1)} %copy.45), calls=%async_computation.1 | async-start | bytes 524288 | tf_op jit(solution)/shard_map/all_to_all | solution.py:25
  80.6 0.1 copy.51
  80.7 0.1 reshape.57
  80.8 0.5 copy.52
  81.3 0.2 reshape.56
  81.4 23.8 %all-to-all-done = bf16[512,1,1,2,128]{4,3,2,1,0:T(2,128)(2,1)S(1)} async-done(((bf16[512,1,1,2,128]{4,3,2,1,0:T(2,128)(2,1)}), bf16[512,1,1,2,128]{4,3,2,1,0:T(2,128)(2,1)S(1)}, u32[]{:S(2)}, u32[]{:S(2)}) %all-to-all-start) | async-done | bytes 262176 | tf_op jit(solution)/shard_map/all_to_all | solution.py:25
  105.3 0.3 copy.47
  105.6 0.2 multiply_reduce_fusion
  105.8 0.5 copy.48
  106.2 0.2 add.50
  106.4 2.1 %fusion.18 = (f32[1024]{0:T(1024)S(1)}, f32[1024,1024]{0,1:T(8,128)S(1)}) fusion(f32[1024]{0:T(1024)S(1)} %reshape.56, f32[1024]{0:T(1024)S(1)} %compare_convert_fusion, bf16[1024,128]{1,0:T(8,128)(2,1)S(1)} %bitcast.52, f32[1024]{0:T(1024)S(1)} %add.50), kind=kOutput, calls=%fused_computation.44 | convolution fusion | flops 279968768 | bytes 4472832 | tf_op jit(solution)/shard_map/dot_general | solution.py:35
  108.5 0.6 divide_convert_fusion
  109.1 0.7 fusion.3
  109.9 0.7 fusion.2
  110.6 0.0 copy-start.1
  110.6 0.3 copy.64
  110.9 1.2 copy.54
  112.1 8.8 %all-to-all-start.2 = ((f32[512,1,1,2,128]{4,3,2,1,0:T(2,128)}), f32[512,1,1,2,128]{4,3,2,1,0:T(2,128)S(1)}, u32[]{:S(2)}, u32[]{:S(2)}) async-start(f32[512,1,1,2,128]{4,3,2,1,0:T(2,128)} %copy.54), calls=%async_computation.3 | async-start | bytes 1048576 | tf_op jit(solution)/shard_map/all_to_all | solution.py:25
  121.0 35.8 %all-to-all-done.2 = f32[512,1,1,2,128]{4,3,2,1,0:T(2,128)S(1)} async-done(((f32[512,1,1,2,128]{4,3,2,1,0:T(2,128)}), f32[512,1,1,2,128]{4,3,2,1,0:T(2,128)S(1)}, u32[]{:S(2)}, u32[]{:S(2)}) %all-to-all-start.2) | async-done | bytes 524320 | tf_op jit(solution)/shard_map/all_to_all | solution.py:25
  156.9 0.4 copy.56
  157.3 1.0 gather_fusion
  158.3 0.0 copy-done.1
  158.3 0.9 convert_select_fusion
  (10 shorter events, 0.1 us)
Async XLA Ops:
  6.5 0.9 copy-start
  6.5 5.7 %copy-start.4 = (bf16[512]{0:T(512)(128)(2,1)S(1)}, bf16[512]{0:T(512)(128)(2,1)}, u32[]{:S(2)}) copy-start(bf16[512]{0:T(512)(128)(2,1)} %param.7) | copy-start | bytes 3076
  6.5 5.7 %copy-start.3 = (s32[512]{0:T(512)S(1)}, s32[512]{0:T(512)}, u32[]{:S(2)}) copy-start(s32[512]{0:T(512)} %param.9) | copy-start | bytes 6148
  6.5 5.7 %copy-start.2 = (s32[512,1]{0,1:T(1,128)S(1)}, s32[512,1]{0,1:T(1,128)}, u32[]{:S(2)}) copy-start(s32[512,1]{0,1:T(1,128)} %param.8) | copy-start | bytes 6148
  6.5 51.4 %reduce-scatter.2.cloned.1.call-start = ((), (), s32[]{:S(2)}) async-start(), calls=%async_computation.4 | async-start | bytes 2359296 | tf_op jit(solution)/shard_map/reduce_scatter | solution.py:60
  14.9 48.9 %all-to-all-start.1 = ((bf16[512,1,1,2]{3,2,1,0:T(2,128)(2,1)}), bf16[512,1,1,2]{3,2,1,0:T(2,128)(2,1)S(1)}, u32[]{:S(2)}, u32[]{:S(2)}) async-start(bf16[512,1,1,2]{3,2,1,0:T(2,128)(2,1)} %copy.50), calls=%async_computation.2 | async-start | bytes 524288 | tf_op jit(solution)/shard_map/all_to_all | solution.py:25
  63.8 41.5 %all-to-all-start = ((bf16[512,1,1,2,128]{4,3,2,1,0:T(2,128)(2,1)}), bf16[512,1,1,2,128]{4,3,2,1,0:T(2,128)(2,1)S(1)}, u32[]{:S(2)}, u32[]{:S(2)}) async-start(bf16[512,1,1,2,128]{4,3,2,1,0:T(2,128)(2,1)} %copy.45), calls=%async_computation.1 | async-start | bytes 524288 | tf_op jit(solution)/shard_map/all_to_all | solution.py:25
  110.6 47.7 %copy-start.1 = (f32[512,128]{1,0:T(8,128)S(1)}, f32[512,128]{1,0:T(8,128)}, u32[]{:S(2)}) copy-start(f32[512,128]{1,0:T(8,128)} %reduce-scatter.2.cloned.1.call-done) | copy-start | bytes 786436
  112.1 44.7 %all-to-all-start.2 = ((f32[512,1,1,2,128]{4,3,2,1,0:T(2,128)}), f32[512,1,1,2,128]{4,3,2,1,0:T(2,128)S(1)}, u32[]{:S(2)}, u32[]{:S(2)}) async-start(f32[512,1,1,2,128]{4,3,2,1,0:T(2,128)} %copy.54), calls=%async_computation.3 | async-start | bytes 1048576 | tf_op jit(solution)/shard_map/all_to_all | solution.py:25
Sparse Core Ops, SparseCore 0:
  12.4 45.5 reduce-scatter.1
where the time goes:
time: 166 us
  waiting for transfers between devices  81.7 us (49%)
  starting transfers between devices  49.9 us (30%)
  between operations  13.6 us (8%)
  matrix products  10.2 us (6%)
  local copies, waits for them, and re-layouts  8.6 us (5%)
  other arithmetic  2.04 us (1%)
    all_to_all x3, waiting for transfers between devices, exchange_both(): parts = lax.all_to_all(parts, axis, split_axis=0, concat_axis=0, tiled=True)  62.9 us
    all_to_all x3, starting transfers between devices, exchange_both(): parts = lax.all_to_all(parts, axis, split_axis=0, concat_axis=0, tiled=True)  49.9 us
    reduce_scatter x1, waiting for transfers between devices, body(): lax.psum_scatter(jnp.dot(expression, loading, preferred_element_type=jnp....  18.8 us
    dot_general x1, matrix products, body(): jnp.dot(expression, loading, preferred_element_type=jnp.float32)  4.77 us
  transfers between devices with their start and end apart: 4, of which 4 were waited for; matrix products, arithmetic and copies ran while one was open for 4% of the time, Pallas kernels for 0%

commit v1 on v0

v1 whole, which is shorter than its diff:
```python
import functools

import jax
import jax.numpy as jnp
from jax import lax
from jax.experimental import pallas as pl
from jax.experimental.pallas import tpu as pltpu
from jax.sharding import PartitionSpec as P

MESH = pl.DeviceIdType.MESH
F32 = jnp.float32
BF16 = jnp.bfloat16
I32 = jnp.int32

X, Z, Y = 4, 16, 4
GROUP = 8
ROWS = 512
HALF = ROWS // 2
COMPS = 128
SLOTS = 1024
CHUNK = 256
PIECE = 32
TILE = 16
DY_ORDER = (2, 1, 3, 0)
DX_ORDER = (2, 1, 3, 0)


def iota(shape, dim):
    return lax.broadcasted_iota(I32, shape, dim)


def dot(a, b):
    return jnp.dot(a, b, preferred_element_type=F32)


def dot_nt(a, b):
    return lax.dot_general(a, b, (((1,), (1,)), ((), ())), preferred_element_type=F32)


def as_columns(row):
    n = row.shape[1]
    return jnp.concatenate(
        [jnp.broadcast_to(row[:, m : m + 128], (128, 128)).T for m in range(0, n, 128)], axis=0
    )


def as_row(columns):
    n = columns.shape[0]
    return jnp.concatenate([columns[m : m + 128, :].T[0:1, :] for m in range(0, n, 128)], axis=1)


def far_first(t):
    return 8 + (1 - 2 * (t % 2)) * ((t + 1) // 2)


def kernel(
    expr, load_ref, width_ref, cluster_ref, quality_ref, out_ref,
    xbuf, sib_out, sib_in, a_out, a_in, b_out, b_in, s_keep, e_keep,
    hot, hot_t, p1, r1, p2, emb, w1, w1_in, w2, w2_in, rw_col, rw_row,
    aff, o_keep, s1_ref, p3, r3, p4, r4,
    x_sem, sib_s, sib_r, a_s, a_r, b_s, b_r, s1_s, s1_r, s2_s, s2_r, s3_s, s3_r, s4_s, s4_r,
    w1_s, w1_r, w2_s, w2_r,
):
    q = lax.axis_index("cells")
    g = lax.axis_index("genes")
    x, z = q // Z, q % Z
    y, core = g // 2, g % 2
    other = 1 - core

    def remote(src, dst, ssem, rsem, dev):
        return pltpu.make_async_remote_copy(
            src_ref=src, dst_ref=dst, send_sem=ssem, recv_sem=rsem,
            device_id=dev, device_id_type=MESH,
        )

    def at_y(dy):
        return (q, ((y + dy) % Y) * 2 + core)

    sibling = (q, y * 2 + other)

    def fetch(i):
        dy, c = DY_ORDER[i % 4], (other if i < 4 else core)
        block = ((y + dy) % Y) * 2 + c
        return pltpu.make_async_copy(
            expr.at[pl.ds(pl.multiple_of(block * ROWS, ROWS), ROWS)], xbuf.at[i], x_sem.at[i]
        )

    for i in range(8):
        fetch(i).start()

    barrier = pltpu.get_barrier_semaphore()

    @pl.loop(1, GROUP)
    def _(d):
        pl.semaphore_signal(barrier, 1, device_id=(q, (g + d) % GROUP), device_id_type=MESH)

    @pl.loop(1, X * Z)
    def _(j):
        dev = (((x + j // Z) % X) * Z + (z + j % Z) % Z, g)
        pl.semaphore_signal(barrier, 1, device_id=dev, device_id_type=MESH)

    loading = load_ref[...]
    for i in range(4):
        fetch(i).wait()
        sib_out[i] = dot(xbuf[i], loading)
        if i == 0:
            pl.semaphore_wait(barrier, GROUP - 1 + X * Z - 1)
        remote(sib_out.at[i], sib_in.at[i], sib_s.at[i], sib_r.at[i], sibling).start()

    def chip_sum(i):
        fetch(4 + i).wait()
        part = dot(xbuf[4 + i], loading)
        remote(sib_out.at[i], sib_in.at[i], sib_s.at[i], sib_r.at[i], sibling).wait_recv()
        return part + sib_in[i]

    up, down = at_y(1), at_y(3)
    low, high = pl.ds(0, HALF), pl.ds(HALF, HALF)
    a_out[...] = chip_sum(0).astype(BF16)
    a_up = remote(a_out.at[low], a_in.at[0], a_s.at[0], a_r.at[0], up)
    a_down = remote(a_out.at[high], a_in.at[1], a_s.at[1], a_r.at[1], down)
    a_up.start()
    a_down.start()
    part = chip_sum(1)
    b_out[0, HALF:, :] = part[HALF:].astype(BF16)
    b_up_high = remote(b_out.at[0, high], b_in.at[0, high], b_s.at[0], b_r.at[0], up)
    b_up_high.start()
    s_keep[0] = part[:HALF]
    part = chip_sum(2)
    b_out[1, :HALF, :] = part[:HALF].astype(BF16)
    b_down_low = remote(b_out.at[1, low], b_in.at[1, low], b_s.at[1], b_r.at[1], down)
    b_down_low.start()
    s_keep[1] = part[HALF:]
    e_keep[...] = chip_sum(3)

    cluster = cluster_ref[...]
    live = quality_ref[...] == 1
    owner = cluster % (X * Z)
    gd = cluster // (X * Z)
    dx = (owner // Z - x + X) % X
    dz = (owner % Z - z + Z) % Z
    key = jnp.where(live, cluster, -1).astype(F32)
    key_col = as_columns(key)
    ranks = []
    for m in range(4):
        row = key[:, m * 128 : m * 128 + 128]
        same = (key_col[m * 128 : m * 128 + 128] == row) & (
            iota((128, 128), 0) < iota((128, 128), 1)
        )
        rank = jnp.sum(same.astype(F32), axis=0, keepdims=True)
        for k in range(m):
            same = key_col[k * 128 : k * 128 + 128] == row
            rank += jnp.sum(same.astype(F32), axis=0, keepdims=True)
        ranks.append(rank)
    rank = jnp.concatenate(ranks, axis=1).astype(I32)
    slot = jnp.where(live, dx * CHUNK + gd * PIECE + dz * 2 + rank, -1)
    place = jnp.where(live, dx * PIECE + dz * 2 + rank, -1)
    width = width_ref[...].astype(F32)
    m1 = jnp.where((iota((16, ROWS), 0) == gd) & live, width, 0.0).astype(BF16)
    m2 = (as_columns(place.astype(F32)).astype(I32) == iota((ROWS, 128), 1)).astype(F32).astype(BF16)
    w1_all = dot(m1, m2)
    for k in range(GROUP):
        w1[k] = w1_all[k : k + 1]
    w1_in[g] = w1[g]

    @pl.loop(1, GROUP)
    def _(d):
        to = (g + d) % GROUP
        remote(w1.at[to], w1_in.at[g], w1_s, w1_r, (q, to)).start()

    a_up.wait_recv()
    b_out[0, :HALF, :] = (s_keep[0] + a_in[0].astype(F32)).astype(BF16)
    b_up_low = remote(b_out.at[0, low], b_in.at[0, low], b_s.at[2], b_r.at[2], up)
    b_up_low.start()
    a_down.wait_recv()
    b_out[1, HALF:, :] = (s_keep[1] + a_in[1].astype(F32)).astype(BF16)
    b_down_high = remote(b_out.at[1, high], b_in.at[1, high], b_s.at[3], b_r.at[3], down)
    b_down_high.start()

    for m in range(4):
        hot[m * CHUNK : (m + 1) * CHUNK, :] = (
            (iota((CHUNK, ROWS), 0) + m * CHUNK == slot).astype(F32).astype(BF16)
        )
    slot_col = as_columns(slot.astype(F32)).astype(I32)
    for m in range(8):
        hot_t[:, m * 128 : (m + 1) * 128] = (
            (slot_col == iota((ROWS, 128), 1) + m * 128).astype(F32).astype(BF16)
        )
    o, i = iota((CHUNK, CHUNK), 0), iota((CHUNK, CHUNK), 1)
    perm = (((o // 2) % 8) * PIECE + (o // TILE) * 2 + o % 2 == i).astype(F32).astype(BF16)
    perm_t = (((i // 2) % 8) * PIECE + (i // TILE) * 2 + i % 2 == o).astype(F32).astype(BF16)

    remote(w1.at[pl.ds(0, 7)], w1_in.at[pl.ds(0, 7)], w1_s, w1_r, sibling).wait_recv()
    w1_rows = jnp.concatenate(
        [w1_in[k] for k in range(GROUP)] + [jnp.zeros((120, 128), F32)], axis=0
    ).astype(BF16)
    w2_all = jnp.zeros((64, 128), F32)
    for r in range(2):
        pick = (iota((64, 128), 0) * 2 + r == iota((64, 128), 1)).astype(F32).astype(BF16)
        put = (iota((128, 128), 0) * 2 + r == iota((128, 128), 1)).astype(F32).astype(BF16)
        w2_all += dot(dot_nt(pick, w1_rows).astype(BF16), put)
    for k in range(64):
        w2[k] = w2_all[k : k + 1]
    w2_in[0] = w2[0]

    b_up_high.wait_recv()
    b_down_low.wait_recv()
    b_up_low.wait_recv()
    b_down_high.wait_recv()
    embedded = e_keep[...] + b_in[0].astype(F32) + b_in[1].astype(F32)
    e_keep[...] = embedded
    e_rows = embedded.astype(BF16)

    for k in DX_ORDER:
        p1[k] = dot(hot[k * CHUNK : (k + 1) * CHUNK, :], e_rows).astype(BF16)

        @pl.loop(1, GROUP)
        def _(d):
            to = (g + d) % GROUP
            remote(
                p1.at[k, pl.ds(pl.multiple_of(to * PIECE, PIECE), PIECE)],
                r1.at[k, pl.ds(pl.multiple_of(g * PIECE, PIECE), PIECE)],
                s1_s.at[k], s1_r.at[k], (q, to),
            ).start()

        mine = pl.ds(pl.multiple_of(g * PIECE, PIECE), PIECE)
        r1[k, mine, :] = p1[k, mine, :]

    @pl.loop(1, X * Z)
    def _(j):
        dev = (((x + j // Z) % X) * Z + (z + j % Z) % Z, g)
        remote(w2.at[j], w2_in.at[j], w2_s, w2_r, dev).start()

    def all_but_one(src, dst, ssem, rsem):
        n = CHUNK - PIECE
        return remote(src.at[pl.ds(0, n)], dst.at[pl.ds(0, n)], ssem, rsem, sibling)

    def tiles(k, src, dst, ssem, rsem):
        n = CHUNK - TILE if k == 0 else CHUNK
        return remote(src.at[pl.ds(0, n)], dst.at[pl.ds(0, n)], ssem, rsem, sibling)

    for k in DX_ORDER:
        all_but_one(p1.at[k], r1.at[k], s1_s.at[k], s1_r.at[k]).wait_recv()
        p2[k] = dot(perm, r1[k]).astype(BF16)

        @pl.loop(0, Z - 1 if k == 0 else Z)
        def _(t):
            d = far_first(t)
            rows = pl.ds(pl.multiple_of(d * TILE, TILE), TILE)
            dev = (((x + k) % X) * Z + (z + d) % Z, g)
            remote(p2.at[k, rows], emb.at[k, rows], s2_s.at[k], s2_r.at[k], dev).start()

        if k == 0:
            emb[0, :TILE, :] = p2[0, :TILE, :]

    remote(w2.at[pl.ds(0, 63)], w2_in.at[pl.ds(0, 63)], w2_s, w2_r, sibling).wait_recv()
    w2_rows = jnp.concatenate(
        [w2_in[k] for k in range(64)] + [jnp.zeros((64, 128), F32)], axis=0
    ).astype(BF16)
    s, lane = iota((SLOTS, 128), 0), iota((SLOTS, 128), 1)
    spread = dot((s // TILE == lane).astype(F32).astype(BF16), w2_rows)
    own = jnp.where(s % TILE == lane, spread, 0.0).astype(BF16)
    w_col = dot(own, jnp.ones((128, 128), BF16))
    rw = jnp.where(w_col > 0, 1.0 / jnp.where(w_col > 0, w_col, 1.0), 0.0)
    rw_col[...] = rw
    rw_row[...] = as_row(rw)

    for k in DX_ORDER:
        tiles(k, p2.at[k], emb.at[k], s2_s.at[k], s2_r.at[k]).wait_recv()

    rows = emb[...].reshape(SLOTS, COMPS)
    wide = rows.astype(F32)
    norm = jnp.broadcast_to(jnp.sum(wide * wide, axis=1, keepdims=True), (SLOTS, 128))
    norm_row = as_row(norm)
    present = (rw_col[...] > 0).astype(F32).astype(BF16)
    with_ones = jnp.concatenate([rows, present], axis=1)
    for k in range(4):
        part = slice(k * CHUNK, (k + 1) * CHUNK)
        products = dot_nt(rows[part], rows)
        distance = norm[part, 0:1] + norm_row - 2.0 * products
        affinity = jnp.exp(-distance * rw_col[part, 0:1] * rw_row[...]).astype(BF16)
        aff[k] = affinity
        both = dot(affinity, with_ones)
        here = rw_col[part, :] > 0
        inverse = jnp.where(here, 1.0 / jnp.where(here, both[:, COMPS:], 1.0), 0.0)
        moved = both[:, :COMPS] * inverse
        o_keep[k] = 0.25 * moved
        rw_col[part, :] = 0.5 * inverse
        s1_ref[part, :] = jnp.where(here, 0.5 * (wide[part] + moved), 0.0).astype(BF16)

    for k in DX_ORDER:
        part = slice(k * CHUNK, (k + 1) * CHUNK)
        p3[k] = (o_keep[k] + rw_col[part, :] * dot(aff[k], s1_ref[...])).astype(BF16)

        @pl.loop(0, Z - 1 if k == 0 else Z)
        def _(t):
            d = far_first(t)
            rows = pl.ds(pl.multiple_of(d * TILE, TILE), TILE)
            dev = (((x - k + X) % X) * Z + (z - d + Z) % Z, g)
            remote(p3.at[k, rows], r3.at[k, rows], s3_s.at[k], s3_r.at[k], dev).start()

        if k == 0:
            r3[0, :TILE, :] = p3[0, :TILE, :]

    for k in DX_ORDER:
        tiles(k, p3.at[k], r3.at[k], s3_s.at[k], s3_r.at[k]).wait_recv()
        p4[k] = dot(perm_t, r3[k]).astype(BF16)

        @pl.loop(1, GROUP)
        def _(d):
            to = (g + d) % GROUP
            remote(
                p4.at[k, pl.ds(pl.multiple_of(to * PIECE, PIECE), PIECE)],
                r4.at[k, pl.ds(pl.multiple_of(g * PIECE, PIECE), PIECE)],
                s4_s.at[k], s4_r.at[k], (q, to),
            ).start()

        mine = pl.ds(pl.multiple_of(g * PIECE, PIECE), PIECE)
        r4[k, mine, :] = p4[k, mine, :]

    live_col = as_columns(quality_ref[...].astype(F32)) == 1.0
    total = jnp.where(live_col, 0.25, 1.0) * e_keep[...]
    for k in DX_ORDER:
        all_but_one(p4.at[k], r4.at[k], s4_s.at[k], s4_r.at[k]).wait_recv()
        total += dot(hot_t[:, k * CHUNK : (k + 1) * CHUNK], r4[k])
    out_ref[...] = total

    for i in range(4):
        remote(sib_out.at[i], sib_in.at[i], sib_s.at[i], sib_r.at[i], sibling).wait_send()
    for copy in (a_up, a_down, b_up_high, b_down_low, b_up_low, b_down_high):
        copy.wait_send()
    remote(w1.at[pl.ds(0, 7)], w1_in.at[pl.ds(0, 7)], w1_s, w1_r, sibling).wait_send()
    remote(w2.at[pl.ds(0, 63)], w2_in.at[pl.ds(0, 63)], w2_s, w2_r, sibling).wait_send()
    for k in DX_ORDER:
        all_but_one(p1.at[k], r1.at[k], s1_s.at[k], s1_r.at[k]).wait_send()
        tiles(k, p2.at[k], emb.at[k], s2_s.at[k], s2_r.at[k]).wait_send()
        tiles(k, p3.at[k], r3.at[k], s3_s.at[k], s3_r.at[k]).wait_send()
        all_but_one(p4.at[k], r4.at[k], s4_s.at[k], s4_r.at[k]).wait_send()


def body(expression, loading, kernel_width, cluster, quality):
    vmem = pl.BlockSpec(memory_space=pltpu.VMEM)
    dma = pltpu.SemaphoreType.DMA
    chunks = pltpu.VMEM((4, CHUNK, COMPS), BF16)
    return pl.pallas_call(
        kernel,
        out_shape=jax.ShapeDtypeStruct((ROWS, COMPS), F32),
        in_specs=[pl.BlockSpec(memory_space=pl.ANY), vmem, vmem, vmem, vmem],
        out_specs=vmem,
        scratch_shapes=[
            pltpu.VMEM((8, ROWS, 512), BF16),
            pltpu.VMEM((4, ROWS, COMPS), F32),
            pltpu.VMEM((4, ROWS, COMPS), F32),
            pltpu.VMEM((ROWS, COMPS), BF16),
            pltpu.VMEM((2, HALF, COMPS), BF16),
            pltpu.VMEM((2, ROWS, COMPS), BF16),
            pltpu.VMEM((2, ROWS, COMPS), BF16),
            pltpu.VMEM((2, HALF, COMPS), F32),
            pltpu.VMEM((ROWS, COMPS), F32),
            pltpu.VMEM((SLOTS, ROWS), BF16),
            pltpu.VMEM((ROWS, SLOTS), BF16),
            chunks,
            chunks,
            chunks,
            chunks,
            pltpu.VMEM((GROUP, 1, 128), F32),
            pltpu.VMEM((GROUP, 1, 128), F32),
            pltpu.VMEM((X * Z, 1, 128), F32),
            pltpu.VMEM((X * Z, 1, 128), F32),
            pltpu.VMEM((SLOTS, 128), F32),
            pltpu.VMEM((1, SLOTS), F32),
            pltpu.VMEM((4, CHUNK, SLOTS), BF16),
            pltpu.VMEM((4, CHUNK, COMPS), F32),
            pltpu.VMEM((SLOTS, COMPS), BF16),
            chunks,
            chunks,
            chunks,
            chunks,
            dma((8,)), dma((4,)), dma((4,)), dma((2,)), dma((2,)), dma((4,)), dma((4,)),
            dma((4,)), dma((4,)), dma((4,)), dma((4,)), dma((4,)), dma((4,)), dma((4,)), dma((4,)),
            dma, dma, dma, dma,
        ],
        compiler_params=pltpu.CompilerParams(
            collective_id=0, has_side_effects=True, vmem_limit_bytes=48 * 1024 * 1024
        ),
    )(
        expression,
        loading,
        kernel_width.reshape(1, ROWS),
        cluster.reshape(1, ROWS),
        quality.reshape(1, ROWS),
    )


def solution(mesh):
    return jax.shard_map(
        body,
        mesh=mesh,
        in_specs=(
            P("cells", "genes"),
            P("genes", None),
            P(("cells", "genes")),
            P(("cells", "genes"), None),
            P(("cells", "genes")),
        ),
        out_specs=P(("cells", "genes"), None),
        check_vma=False,
    )
```

time: 166 us -> 78.5 us (0.47)
  waiting for transfers between devices: 81.7 us -> 0 us
  Pallas kernels: 0 us -> 72.5 us
  starting transfers between devices: 49.9 us -> 0 us
  between operations: 13.6 us -> 0.01 us
  matrix products: 10.2 us -> 0 us
  local copies, waits for them, and re-layouts: 8.6 us -> 5.84 us
  other arithmetic: 2.04 us -> 0 us
    pallas_call x0 -> x1, Pallas kernels: none -> 72.5 us  [body(): pl.pallas_call(kernel, out_shape=jax.ShapeDtypeStruct((ROWS, COMPS), F32)...]
    all_to_all x3 -> x0, waiting for transfers between devices: 62.9 us -> none  [exchange_both(): parts = lax.all_to_all(parts, axis, split_axis=0, concat_axis=0, tiled=True)]
    all_to_all x3 -> x0, starting transfers between devices: 49.9 us -> none  [exchange_both(): parts = lax.all_to_all(parts, axis, split_axis=0, concat_axis=0, tiled=True)]
    reduce_scatter x1 -> x0, waiting for transfers between devices: 18.8 us -> none  [body(): lax.psum_scatter(jnp.dot(expression, loading, preferred_element_type=jnp....]
    dot_general x6 -> x0, matrix products: 10.2 us -> none  [the longest x1 4.77 us: body(): jnp.dot(expression, loading, preferred_element_type=jnp.float32)]
    unnamed x11 -> x9, local copies, waits for them, and re-layouts: 0.88 us -> 5.16 us
    another operation x7 -> x0, local copies, waits for them, and re-layouts: 3.94 us -> none  [the longest x4 3.19 us: exchange_both(): parts = parts.reshape(-1, *inside)]
  transfers between devices with their start and end apart: 4 -> 0, of which waited for: 4 -> 0; matrix products, arithmetic and copies ran while one was open for 4% -> 0% of each run, Pallas kernels for 0% -> 0%
where the time goes in v1:
time: 78.5 us; the launch traced here: 78.3 us
  Pallas kernels  72.5 us (92%)
  local copies, waits for them, and re-layouts  5.84 us (7%)
    pallas_call x1, Pallas kernels, body(): pl.pallas_call(kernel, out_shape=jax.ShapeDtypeStruct((ROWS, COMPS), F32)...  72.5 us
    unnamed x9, local copies, waits for them, and re-layouts  5.16 us

profile of v1, /device:TPU:1, one launch (start us, length us, event | category | flops | bytes accessed | tf_op | source)
XLA Modules:
  0.0 78.3 jit_solution(10316557908869588207)
XLA Ops:
  0.0 0.7 reshape.9.width_ref
  0.7 0.0 copy-start
  0.7 2.2 %copy-done = bf16[4096,512]{1,0:T(8,128)(2,1)S(1)} copy-done((bf16[4096,512]{1,0:T(8,128)(2,1)S(1)}, bf16[4096,512]{1,0:T(8,128)(2,1)}, u32[]{:S(2)}) %copy-start) | copy-done | bytes 4194328
  2.9 0.0 copy-start.1
  2.9 0.9 %copy-done.1 = bf16[512,128]{1,0:T(8,128)(2,1)S(1)} copy-done((bf16[512,128]{1,0:T(8,128)(2,1)S(1)}, bf16[512,128]{1,0:T(8,128)(2,1)}, u32[]{:S(2)}) %copy-start.1) | copy-done | bytes 131096
  3.8 0.0 copy-start.2
  3.8 0.7 copy-done.2
  4.5 0.0 copy-start.3
  4.5 0.7 copy-done.3
  5.1 72.5 %shard_map.55 = f32[512,128]{1,0:T(8,128)S(1)} custom-call(bf16[4096,512]{1,0:T(8,128)(2,1)S(1)} %copy-done, bf16[512,128]{1,0:T(8,128)(2,1)S(1)} %copy-done.1, bf16[1,512]{1,0:T(2,128)(2,1)S(1)} %reshape.9.width_ref, s32[1,512]{1,0:T(1,128)S(1)} %bitcast.2, s32[1,512]{1,0:T(1,128)S(1)} %bitcast.3), custom_call_target="tpu_custom_call" | custom-call | tf_op jit(solution)/shard_map/pallas_call | solution.py:344
  77.6 0.7 copy.7
Async XLA Ops:
  0.7 2.2 %copy-start = (bf16[4096,512]{1,0:T(8,128)(2,1)S(1)}, bf16[4096,512]{1,0:T(8,128)(2,1)}, u32[]{:S(2)}) copy-start(bf16[4096,512]{1,0:T(8,128)(2,1)} %expr.1) | copy-start | bytes 12582916
  2.9 0.9 %copy-start.1 = (bf16[512,128]{1,0:T(8,128)(2,1)S(1)}, bf16[512,128]{1,0:T(8,128)(2,1)}, u32[]{:S(2)}) copy-start(bf16[512,128]{1,0:T(8,128)(2,1)} %load_ref.1) | copy-start | bytes 393220
  3.8 0.7 copy-start.2
  4.5 0.7 copy-start.3

commit v2 on v1

--- a/solution.py
+++ b/solution.py
@@ -54,12 +54,12 @@
 
 
 def kernel(
-    expr, load_ref, width_ref, cluster_ref, quality_ref, out_ref,
-    xbuf, sib_out, sib_in, a_out, a_in, b_out, b_in, s_keep, e_keep,
-    hot, hot_t, p1, r1, p2, emb, w1, w1_in, w2, w2_in, rw_col, rw_row,
+    expr, load_hbm, width_hbm, cluster_hbm, quality_hbm, out_ref,
+    xbuf, parts, perm_t, load_ref, width_ref, cluster_ref, quality_ref, sib_out, sib_in, a_out, a_in, b_out, b_in, s_keep, e_keep,
+    hot, hot_t, p1, r1, p2, emb, w1, w1_in, w2, wx, w2_in, rw_col, rw_row,
     aff, o_keep, s1_ref, p3, r3, p4, r4,
-    x_sem, sib_s, sib_r, a_s, a_r, b_s, b_r, s1_s, s1_r, s2_s, s2_r, s3_s, s3_r, s4_s, s4_r,
-    w1_s, w1_r, w2_s, w2_r,
+    x_sem, in_sem, sib_s, sib_r, a_s, a_r, b_s, b_r, s1_s, s1_r, s2_s, s2_r, s3_s, s3_r, s4_s, s4_r,
+    w1_s, w1_r, wx_s, wx_r, w2_s, w2_r,
 ):
     q = lax.axis_index("cells")
     g = lax.axis_index("genes")
@@ -77,6 +77,11 @@
         return (q, ((y + dy) % Y) * 2 + core)
 
     sibling = (q, y * 2 + other)
+    sent = []
+
+    def finish():
+        for copy in sent:
+            copy.wait_send()
 
     def fetch(i):
         dy, c = DY_ORDER[i % 4], (other if i < 4 else core)
@@ -85,33 +90,50 @@
             expr.at[pl.ds(pl.multiple_of(block * ROWS, ROWS), ROWS)], xbuf.at[i], x_sem.at[i]
         )
 
+    small = [
+        pltpu.make_async_copy(src, dst, in_sem.at[i])
+        for i, (src, dst) in enumerate(
+            [
+                (load_hbm, load_ref),
+                (cluster_hbm, cluster_ref),
+                (quality_hbm, quality_ref),
+                (width_hbm, width_ref),
+            ]
+        )
+    ]
+    small[0].start()
     for i in range(8):
         fetch(i).start()
+    for copy in small[1:]:
+        copy.start()
 
     barrier = pltpu.get_barrier_semaphore()
+
+    @pl.loop(0, X * Z - 1)
+    def _(j):
+        dev = (((x + 1 + j % X) % X) * Z + (z + far_first(j // X)) % Z, g)
+        pl.semaphore_signal(barrier, 1, device_id=dev, device_id_type=MESH)
 
     @pl.loop(1, GROUP)
     def _(d):
         pl.semaphore_signal(barrier, 1, device_id=(q, (g + d) % GROUP), device_id_type=MESH)
 
-    @pl.loop(1, X * Z)
-    def _(j):
-        dev = (((x + j // Z) % X) * Z + (z + j % Z) % Z, g)
-        pl.semaphore_signal(barrier, 1, device_id=dev, device_id_type=MESH)
-
+    small[0].wait()
     loading = load_ref[...]
     for i in range(4):
         fetch(i).wait()
         sib_out[i] = dot(xbuf[i], loading)
-        if i == 0:
-            pl.semaphore_wait(barrier, GROUP - 1 + X * Z - 1)
-        remote(sib_out.at[i], sib_in.at[i], sib_s.at[i], sib_r.at[i], sibling).start()
+    for i in range(4):
+        fetch(4 + i).wait()
+        parts[i] = dot(xbuf[4 + i], loading)
+    pl.semaphore_wait(barrier, GROUP - 1 + X * Z - 1)
+    for i in range(4):
+        sent.append(remote(sib_out.at[i], sib_in.at[i], sib_s.at[i], sib_r.at[i], sibling))
+        sent[-1].start()
 
     def chip_sum(i):
-        fetch(4 + i).wait()
-        part = dot(xbuf[4 + i], loading)
-        remote(sib_out.at[i], sib_in.at[i], sib_s.at[i], sib_r.at[i], sibling).wait_recv()
-        return part + sib_in[i]
+        sent[i].wait_recv()
+        return parts[i] + sib_in[i]
 
     up, down = at_y(1), at_y(3)
     low, high = pl.ds(0, HALF), pl.ds(HALF, HALF)
@@ -119,19 +141,25 @@
     a_up = remote(a_out.at[low], a_in.at[0], a_s.at[0], a_r.at[0], up)
     a_down = remote(a_out.at[high], a_in.at[1], a_s.at[1], a_r.at[1], down)
     a_up.start()
+    sent.append(a_up)
     a_down.start()
+    sent.append(a_down)
     part = chip_sum(1)
     b_out[0, HALF:, :] = part[HALF:].astype(BF16)
     b_up_high = remote(b_out.at[0, high], b_in.at[0, high], b_s.at[0], b_r.at[0], up)
     b_up_high.start()
+    sent.append(b_up_high)
     s_keep[0] = part[:HALF]
     part = chip_sum(2)
     b_out[1, :HALF, :] = part[:HALF].astype(BF16)
     b_down_low = remote(b_out.at[1, low], b_in.at[1, low], b_s.at[1], b_r.at[1], down)
     b_down_low.start()
+    sent.append(b_down_low)
     s_keep[1] = part[HALF:]
     e_keep[...] = chip_sum(3)
 
+    for copy in small[1:]:
+        copy.wait()
     cluster = cluster_ref[...]
     live = quality_ref[...] == 1
     owner = cluster % (X * Z)
@@ -154,7 +182,7 @@
     rank = jnp.concatenate(ranks, axis=1).astype(I32)
     slot = jnp.where(live, dx * CHUNK + gd * PIECE + dz * 2 + rank, -1)
     place = jnp.where(live, dx * PIECE + dz * 2 + rank, -1)
-    width = width_ref[...].astype(F32)
+    width = width_ref[...].reshape(1, ROWS).astype(F32)
     m1 = jnp.where((iota((16, ROWS), 0) == gd) & live, width, 0.0).astype(BF16)
     m2 = (as_columns(place.astype(F32)).astype(I32) == iota((ROWS, 128), 1)).astype(F32).astype(BF16)
     w1_all = dot(m1, m2)
@@ -167,29 +195,27 @@
         to = (g + d) % GROUP
         remote(w1.at[to], w1_in.at[g], w1_s, w1_r, (q, to)).start()
 
+    for m in range(4):
+        hot[m * CHUNK : (m + 1) * CHUNK, :] = (
+            (iota((CHUNK, ROWS), 0) + m * CHUNK == slot).astype(F32).astype(BF16)
+        )
+    w1_group = remote(w1.at[pl.ds(0, 7)], w1_in.at[pl.ds(0, 7)], w1_s, w1_r, sibling)
+    sent.append(w1_group)
     a_up.wait_recv()
     b_out[0, :HALF, :] = (s_keep[0] + a_in[0].astype(F32)).astype(BF16)
     b_up_low = remote(b_out.at[0, low], b_in.at[0, low], b_s.at[2], b_r.at[2], up)
     b_up_low.start()
+    sent.append(b_up_low)
     a_down.wait_recv()
     b_out[1, HALF:, :] = (s_keep[1] + a_in[1].astype(F32)).astype(BF16)
     b_down_high = remote(b_out.at[1, high], b_in.at[1, high], b_s.at[3], b_r.at[3], down)
     b_down_high.start()
-
-    for m in range(4):
-        hot[m * CHUNK : (m + 1) * CHUNK, :] = (
-            (iota((CHUNK, ROWS), 0) + m * CHUNK == slot).astype(F32).astype(BF16)
-        )
-    slot_col = as_columns(slot.astype(F32)).astype(I32)
-    for m in range(8):
-        hot_t[:, m * 128 : (m + 1) * 128] = (
-            (slot_col == iota((ROWS, 128), 1) + m * 128).astype(F32).astype(BF16)
-        )
+    sent.append(b_down_high)
+
     o, i = iota((CHUNK, CHUNK), 0), iota((CHUNK, CHUNK), 1)
     perm = (((o // 2) % 8) * PIECE + (o // TILE) * 2 + o % 2 == i).astype(F32).astype(BF16)
-    perm_t = (((i // 2) % 8) * PIECE + (i // TILE) * 2 + i % 2 == o).astype(F32).astype(BF16)
-
-    remote(w1.at[pl.ds(0, 7)], w1_in.at[pl.ds(0, 7)], w1_s, w1_r, sibling).wait_recv()
+
+    w1_group.wait_recv()
     w1_rows = jnp.concatenate(
         [w1_in[k] for k in range(GROUP)] + [jnp.zeros((120, 128), F32)], axis=0
     ).astype(BF16)
@@ -199,8 +225,15 @@
         put = (iota((128, 128), 0) * 2 + r == iota((128, 128), 1)).astype(F32).astype(BF16)
         w2_all += dot(dot_nt(pick, w1_rows).astype(BF16), put)
     for k in range(64):
-        w2[k] = w2_all[k : k + 1]
-    w2_in[0] = w2[0]
+        w2[k // Z, k % Z] = w2_all[k : k + 1]
+    for k in range(Z):
+        wx[0, k] = w2[0, k]
+    for k in range(1, X):
+        sent.append(
+            remote(w2.at[k], wx.at[k], wx_s.at[k], wx_r.at[k], (((x + k) % X) * Z + z, g))
+        )
+        sent[-1].start()
+    wx_copies = sent[-3:]
 
     b_up_high.wait_recv()
     b_down_low.wait_recv()
@@ -225,10 +258,18 @@
         mine = pl.ds(pl.multiple_of(g * PIECE, PIECE), PIECE)
         r1[k, mine, :] = p1[k, mine, :]
 
-    @pl.loop(1, X * Z)
-    def _(j):
-        dev = (((x + j // Z) % X) * Z + (z + j % Z) % Z, g)
-        remote(w2.at[j], w2_in.at[j], w2_s, w2_r, dev).start()
+    for copy in wx_copies:
+        copy.wait_recv()
+    for k in range(X):
+        w2_in[k, 0] = wx[k, 0]
+
+    @pl.loop(0, Z - 1)
+    def _(t):
+        d = far_first(t)
+        remote(wx.at[:, d], w2_in.at[:, d], w2_s, w2_r, (x * Z + (z + d) % Z, g)).start()
+
+    w2_group = remote(wx.at[:, pl.ds(0, Z - 1)], w2_in.at[:, pl.ds(0, Z - 1)], w2_s, w2_r, sibling)
+    sent.append(w2_group)
 
     def all_but_one(src, dst, ssem, rsem):
         n = CHUNK - PIECE
@@ -239,7 +280,9 @@
         return remote(src.at[pl.ds(0, n)], dst.at[pl.ds(0, n)], ssem, rsem, sibling)
 
     for k in DX_ORDER:
-        all_but_one(p1.at[k], r1.at[k], s1_s.at[k], s1_r.at[k]).wait_recv()
+        arrived = all_but_one(p1.at[k], r1.at[k], s1_s.at[k], s1_r.at[k])
+        arrived.wait_recv()
+        sent.append(arrived)
         p2[k] = dot(perm, r1[k]).astype(BF16)
 
         @pl.loop(0, Z - 1 if k == 0 else Z)
@@ -252,9 +295,18 @@
         if k == 0:
             emb[0, :TILE, :] = p2[0, :TILE, :]
 
-    remote(w2.at[pl.ds(0, 63)], w2_in.at[pl.ds(0, 63)], w2_s, w2_r, sibling).wait_recv()
+    slot_col = as_columns(slot.astype(F32)).astype(I32)
+    for m in range(8):
+        hot_t[:, m * 128 : (m + 1) * 128] = (
+            (slot_col == iota((ROWS, 128), 1) + m * 128).astype(F32).astype(BF16)
+        )
+    perm_t[...] = (((i // 2) % 8) * PIECE + (i // TILE) * 2 + i % 2 == o).astype(F32).astype(BF16)
+    live_col = as_columns(live.astype(F32)) == 1.0
+    e_keep[...] = jnp.where(live_col, 0.25, 1.0) * e_keep[...]
+
+    w2_group.wait_recv()
     w2_rows = jnp.concatenate(
-        [w2_in[k] for k in range(64)] + [jnp.zeros((64, 128), F32)], axis=0
+        [w2_in[k // Z, k % Z] for k in range(64)] + [jnp.zeros((64, 128), F32)], axis=0
     ).astype(BF16)
     s, lane = iota((SLOTS, 128), 0), iota((SLOTS, 128), 1)
     spread = dot((s // TILE == lane).astype(F32).astype(BF16), w2_rows)
@@ -265,7 +317,9 @@
     rw_row[...] = as_row(rw)
 
     for k in DX_ORDER:
-        tiles(k, p2.at[k], emb.at[k], s2_s.at[k], s2_r.at[k]).wait_recv()
+        arrived = tiles(k, p2.at[k], emb.at[k], s2_s.at[k], s2_r.at[k])
+        arrived.wait_recv()
+        sent.append(arrived)
 
     rows = emb[...].reshape(SLOTS, COMPS)
     wide = rows.astype(F32)
@@ -302,8 +356,10 @@
             r3[0, :TILE, :] = p3[0, :TILE, :]
 
     for k in DX_ORDER:
-        tiles(k, p3.at[k], r3.at[k], s3_s.at[k], s3_r.at[k]).wait_recv()
-        p4[k] = dot(perm_t, r3[k]).astype(BF16)
+        arrived = tiles(k, p3.at[k], r3.at[k], s3_s.at[k], s3_r.at[k])
+        arrived.wait_recv()
+        sent.append(arrived)
+        p4[k] = dot(perm_t[...], r3[k]).astype(BF16)
 
         @pl.loop(1, GROUP)
         def _(d):
@@ -317,37 +373,45 @@
         mine = pl.ds(pl.multiple_of(g * PIECE, PIECE), PIECE)
         r4[k, mine, :] = p4[k, mine, :]
 
-    live_col = as_columns(quality_ref[...].astype(F32)) == 1.0
-    total = jnp.where(live_col, 0.25, 1.0) * e_keep[...]
-    for k in DX_ORDER:
-        all_but_one(p4.at[k], r4.at[k], s4_s.at[k], s4_r.at[k]).wait_recv()
+    total = e_keep[...]
+    for k in DX_ORDER:
+        arrived = all_but_one(p4.at[k], r4.at[k], s4_s.at[k], s4_r.at[k])
+        arrived.wait_recv()
+        sent.append(arrived)
         total += dot(hot_t[:, k * CHUNK : (k + 1) * CHUNK], r4[k])
     out_ref[...] = total
 
-    for i in range(4):
-        remote(sib_out.at[i], sib_in.at[i], sib_s.at[i], sib_r.at[i], sibling).wait_send()
-    for copy in (a_up, a_down, b_up_high, b_down_low, b_up_low, b_down_high):
-        copy.wait_send()
-    remote(w1.at[pl.ds(0, 7)], w1_in.at[pl.ds(0, 7)], w1_s, w1_r, sibling).wait_send()
-    remote(w2.at[pl.ds(0, 63)], w2_in.at[pl.ds(0, 63)], w2_s, w2_r, sibling).wait_send()
-    for k in DX_ORDER:
-        all_but_one(p1.at[k], r1.at[k], s1_s.at[k], s1_r.at[k]).wait_send()
-        tiles(k, p2.at[k], emb.at[k], s2_s.at[k], s2_r.at[k]).wait_send()
-        tiles(k, p3.at[k], r3.at[k], s3_s.at[k], s3_r.at[k]).wait_send()
-        all_but_one(p4.at[k], r4.at[k], s4_s.at[k], s4_r.at[k]).wait_send()
+    finish()
 
 
 def body(expression, loading, kernel_width, cluster, quality):
+    hbm = pl.BlockSpec(memory_space=pltpu.HBM)
     vmem = pl.BlockSpec(memory_space=pltpu.VMEM)
     dma = pltpu.SemaphoreType.DMA
     chunks = pltpu.VMEM((4, CHUNK, COMPS), BF16)
+    operands = [
+        pltpu.with_memory_space_constraint(a, pltpu.HBM)
+        for a in (
+            expression,
+            loading,
+            kernel_width,
+            cluster.reshape(1, ROWS),
+            quality.reshape(1, ROWS),
+        )
+    ]
     return pl.pallas_call(
         kernel,
         out_shape=jax.ShapeDtypeStruct((ROWS, COMPS), F32),
-        in_specs=[pl.BlockSpec(memory_space=pl.ANY), vmem, vmem, vmem, vmem],
+        in_specs=[hbm] * 5,
         out_specs=vmem,
         scratch_shapes=[
             pltpu.VMEM((8, ROWS, 512), BF16),
+            pltpu.VMEM((4, ROWS, COMPS), F32),
+            pltpu.VMEM((CHUNK, CHUNK), BF16),
+            pltpu.VMEM((512, COMPS), BF16),
+            pltpu.VMEM((ROWS,), BF16),
+            pltpu.VMEM((1, ROWS), I32),
+            pltpu.VMEM((1, ROWS), I32),
             pltpu.VMEM((4, ROWS, COMPS), F32),
             pltpu.VMEM((4, ROWS, COMPS), F32),
             pltpu.VMEM((ROWS, COMPS), BF16),
@@ -364,8 +428,9 @@
             chunks,
             pltpu.VMEM((GROUP, 1, 128), F32),
             pltpu.VMEM((GROUP, 1, 128), F32),
-            pltpu.VMEM((X * Z, 1, 128), F32),
-            pltpu.VMEM((X * Z, 1, 128), F32),
+            pltpu.VMEM((X, Z, 1, 128), F32),
+            pltpu.VMEM((X, Z, 1, 128), F32),
+            pltpu.VMEM((X, Z, 1, 128), F32),
             pltpu.VMEM((SLOTS, 128), F32),
             pltpu.VMEM((1, SLOTS), F32),
             pltpu.VMEM((4, CHUNK, SLOTS), BF16),
@@ -375,20 +440,14 @@
             chunks,
             chunks,
             chunks,
-            dma((8,)), dma((4,)), dma((4,)), dma((2,)), dma((2,)), dma((4,)), dma((4,)),
+            dma((8,)), dma((4,)), dma((4,)), dma((4,)), dma((2,)), dma((2,)), dma((4,)), dma((4,)),
             dma((4,)), dma((4,)), dma((4,)), dma((4,)), dma((4,)), dma((4,)), dma((4,)), dma((4,)),
-            dma, dma, dma, dma,
+            dma, dma, dma((4,)), dma((4,)), dma, dma,
         ],
         compiler_params=pltpu.CompilerParams(
             collective_id=0, has_side_effects=True, vmem_limit_bytes=48 * 1024 * 1024
         ),
-    )(
-        expression,
-        loading,
-        kernel_width.reshape(1, ROWS),
-        cluster.reshape(1, ROWS),
-        quality.reshape(1, ROWS),
-    )
+    )(*operands)
 
 
 def solution(mesh):

time: 78.5 us -> 70.9 us (0.903)
  local copies, waits for them, and re-layouts: 5.84 us -> 0.71 us
  Pallas kernels: 72.5 us -> 70.1 us
    unnamed x9 -> x1, local copies, waits for them, and re-layouts: 5.16 us -> 0.71 us
    pallas_call x1, Pallas kernels: 72.5 us -> 70.1 us  [body(): pl.pallas_call(kernel, out_shape=jax.ShapeDtypeStruct((ROWS, COMPS), F32)...]
where the time goes in v2:
time: 70.9 us; the launch traced here: 70.8 us
  Pallas kernels  70.1 us (99%)
  local copies, waits for them, and re-layouts  0.71 us (1%)
    pallas_call x1, Pallas kernels, body(): pl.pallas_call(kernel, out_shape=jax.ShapeDtypeStruct((ROWS, COMPS), F32)...  70.1 us

profile of v2, /device:TPU:1, one launch (start us, length us, event | category | flops | bytes accessed | tf_op | source)
XLA Modules:
  0.0 70.8 jit_solution(5832361316101157536)
XLA Ops:
  0.0 70.1 %shard_map.55 = f32[512,128]{1,0:T(8,128)S(1)} custom-call(bf16[4096,512]{1,0:T(8,128)(2,1)} %expr.1, bf16[512,128]{1,0:T(8,128)(2,1)} %load_hbm.1, bf16[512]{0:T(512)(128)(2,1)} %width_hbm.1, s32[1,512]{1,0:T(1,128)} %bitcast.2, s32[1,512]{1,0:T(1,128)} %bitcast.3), custom_call_target="tpu_custom_call" | custom-call | tf_op jit(solution)/shard_map/pallas_call | solution.py:402
  70.1 0.7 copy.7

commit v3 on v2

v3 whole, which is shorter than its diff:
```python
import functools

import jax
import jax.numpy as jnp
from jax import lax
from jax.experimental import pallas as pl
from jax.experimental.pallas import tpu as pltpu
from jax.sharding import PartitionSpec as P

MESH = pl.DeviceIdType.MESH
F32 = jnp.float32
BF16 = jnp.bfloat16
I32 = jnp.int32

X, Z, Y = 4, 16, 4
GROUP = 8
ROWS = 512
HALF = ROWS // 2
COMPS = 128
SLOTS = 1024
CHUNK = 256
PIECE = 32
TILE = 16
DY_ORDER = (2, 1, 3, 0)
OUT_ORDER = (0, 1, 3, 2)
BACK_ORDER = (2, 1, 3, 0)


def iota(shape, dim):
    return lax.broadcasted_iota(I32, shape, dim)


def dot(a, b):
    return jnp.dot(a, b, preferred_element_type=F32)


def dot_nt(a, b):
    return lax.dot_general(a, b, (((1,), (1,)), ((), ())), preferred_element_type=F32)


def as_columns(row):
    n = row.shape[1]
    return jnp.concatenate(
        [jnp.broadcast_to(row[:, m : m + 128], (128, 128)).T for m in range(0, n, 128)], axis=0
    )


def as_row(columns):
    n = columns.shape[0]
    return jnp.concatenate([columns[m : m + 128, :].T[0:1, :] for m in range(0, n, 128)], axis=1)


def far_first(t):
    return 8 + (1 - 2 * (t % 2)) * ((t + 1) // 2)


def near(d):
    return 4 + (2 * (d % 2) - 1) * (d // 2) + 4 * (1 - (d + 7) // 8)


def kernel(
    expr, load_hbm, width_hbm, cluster_hbm, quality_hbm, out_ref,
    xbuf, parts, perm_t, load_ref, width_ref, cluster_ref, quality_ref, sib_out, sib_in, a_out, a_in, b_out, b_in, s_keep, e_keep,
    hot, hot_t, p1, r1, p2, emb, w1, w1_in, w2, wx, wz, w2_in, rw_col, rw_row,
    aff, norm_col, norm_row, ones, both, o_keep, s1_ref, p3, rz, p4, r4,
    x_sem, in_sem, sib_s, sib_r, a_s, a_r, b_s, b_r, s1_s, s1_r, s2_s, s2_r, s3_s, s3_r, s4_s, s4_r,
    w1_s, w1_r, wx_s, wx_r, w2_s, w2_r,
):
    q = lax.axis_index("cells")
    g = lax.axis_index("genes")
    x, z = q // Z, q % Z
    y, core = g // 2, g % 2
    other = 1 - core

    def remote(src, dst, ssem, rsem, dev):
        return pltpu.make_async_remote_copy(
            src_ref=src, dst_ref=dst, send_sem=ssem, recv_sem=rsem,
            device_id=dev, device_id_type=MESH,
        )

    def at_y(dy):
        return (q, ((y + dy) % Y) * 2 + core)

    sibling = (q, y * 2 + other)
    sent = []

    def finish():
        for copy in sent:
            copy.wait_send()

    def fetch(i):
        dy, c = DY_ORDER[i % 4], (other if i < 4 else core)
        block = ((y + dy) % Y) * 2 + c
        return pltpu.make_async_copy(
            expr.at[pl.ds(pl.multiple_of(block * ROWS, ROWS), ROWS)], xbuf.at[i], x_sem.at[i]
        )

    small = [
        pltpu.make_async_copy(src, dst, in_sem.at[i])
        for i, (src, dst) in enumerate(
            [
                (load_hbm, load_ref),
                (cluster_hbm, cluster_ref),
                (quality_hbm, quality_ref),
                (width_hbm, width_ref),
            ]
        )
    ]
    small[0].start()
    for i in range(4):
        fetch(i).start()
        fetch(4 + i).start()
    for copy in small[1:]:
        copy.start()

    barrier = pltpu.get_barrier_semaphore()

    def along_z(d):
        return (x * Z + (z + d + Z) % Z, g)

    def in_plane(k, to):
        return (((x + k + X) % X) * Z + z, to)

    @pl.loop(0, Z - 1)
    def _(t):
        pl.semaphore_signal(barrier, 1, device_id=along_z(far_first(t)), device_id_type=MESH)

    @pl.loop(1, X * GROUP)
    def _(n):
        dev = in_plane(n // GROUP, (g + n) % GROUP)
        pl.semaphore_signal(barrier, 1, device_id=dev, device_id_type=MESH)

    small[0].wait()
    loading = load_ref[...]
    sib_copies = [
        remote(sib_out.at[i], sib_in.at[i], sib_s.at[i], sib_r.at[i], sibling) for i in range(4)
    ]
    sent.extend(sib_copies)

    def for_sibling(i):
        fetch(i).wait()
        sib_out[i] = dot(xbuf[i], loading).astype(BF16)

    def for_own(i):
        fetch(4 + i).wait()
        parts[i] = dot(xbuf[4 + i], loading)

    def chip_sum(i):
        sib_copies[i].wait_recv()
        return parts[i] + sib_in[i].astype(F32)

    for_sibling(0)
    pl.semaphore_wait(barrier, Z - 1 + X * GROUP - 1)
    sib_copies[0].start()
    for_own(0)
    for_sibling(1)
    sib_copies[1].start()

    up, down = at_y(1), at_y(3)
    low, high = pl.ds(0, HALF), pl.ds(HALF, HALF)
    a_out[...] = chip_sum(0).astype(BF16)
    a_up = remote(a_out.at[low], a_in.at[0], a_s.at[0], a_r.at[0], up)
    a_down = remote(a_out.at[high], a_in.at[1], a_s.at[1], a_r.at[1], down)
    a_up.start()
    sent.append(a_up)
    a_down.start()
    sent.append(a_down)
    for_own(1)
    for_sibling(2)
    sib_copies[2].start()
    part = chip_sum(1)
    b_out[0, HALF:, :] = part[HALF:].astype(BF16)
    b_up_high = remote(b_out.at[0, high], b_in.at[0, high], b_s.at[0], b_r.at[0], up)
    b_up_high.start()
    sent.append(b_up_high)
    s_keep[0] = part[:HALF]
    for_own(2)
    for_sibling(3)
    sib_copies[3].start()
    part = chip_sum(2)
    b_out[1, :HALF, :] = part[:HALF].astype(BF16)
    b_down_low = remote(b_out.at[1, low], b_in.at[1, low], b_s.at[1], b_r.at[1], down)
    b_down_low.start()
    sent.append(b_down_low)
    s_keep[1] = part[HALF:]
    for_own(3)

    for copy in small[1:]:
        copy.wait()
    cluster = cluster_ref[...]
    live = quality_ref[...] == 1
    owner = cluster % (X * Z)
    gd = cluster // (X * Z)
    dx = (owner // Z - x + X) % X
    dz = (owner % Z - z + Z) % Z
    key = jnp.where(live, cluster, -1).astype(F32)
    key_col = as_columns(key)
    ranks = []
    for m in range(4):
        row = key[:, m * 128 : m * 128 + 128]
        same = (key_col[m * 128 : m * 128 + 128] == row) & (
            iota((128, 128), 0) < iota((128, 128), 1)
        )
        rank = jnp.sum(same.astype(F32), axis=0, keepdims=True)
        for k in range(m):
            same = key_col[k * 128 : k * 128 + 128] == row
            rank += jnp.sum(same.astype(F32), axis=0, keepdims=True)
        ranks.append(rank)
    rank = jnp.concatenate(ranks, axis=1).astype(I32)
    slot = jnp.where(live, dx * CHUNK + gd * PIECE + dz * 2 + rank, -1)
    place = jnp.where(live, dx * PIECE + dz * 2 + rank, -1)
    a_up.wait_recv()
    b_out[0, :HALF, :] = (s_keep[0] + a_in[0].astype(F32)).astype(BF16)
    b_up_low = remote(b_out.at[0, low], b_in.at[0, low], b_s.at[2], b_r.at[2], up)
    b_up_low.start()
    sent.append(b_up_low)
    a_down.wait_recv()
    b_out[1, HALF:, :] = (s_keep[1] + a_in[1].astype(F32)).astype(BF16)
    b_down_high = remote(b_out.at[1, high], b_in.at[1, high], b_s.at[3], b_r.at[3], down)
    b_down_high.start()
    sent.append(b_down_high)

    width = width_ref[...].reshape(1, ROWS).astype(F32)
    m1 = jnp.where((iota((16, ROWS), 0) == gd) & live, width, 0.0).astype(BF16)
    m2 = (as_columns(place.astype(F32)).astype(I32) == iota((ROWS, 128), 1)).astype(F32).astype(BF16)
    w1_all = dot(m1, m2)
    for k in range(GROUP):
        w1[k] = w1_all[k : k + 1]
    w1_in[g] = w1[g]

    @pl.loop(1, GROUP)
    def _(d):
        to = (g + near(d)) % GROUP
        remote(w1.at[to], w1_in.at[g], w1_s, w1_r, (q, to)).start()

    for m in range(4):
        hot[m * CHUNK : (m + 1) * CHUNK, :] = (
            (iota((CHUNK, ROWS), 0) + m * CHUNK == slot).astype(F32).astype(BF16)
        )
    w1_group = remote(w1.at[pl.ds(0, 7)], w1_in.at[pl.ds(0, 7)], w1_s, w1_r, sibling)
    sent.append(w1_group)
    o, i = iota((CHUNK, CHUNK), 0), iota((CHUNK, CHUNK), 1)
    perm = (((o // 2) % 8) * PIECE + (o // TILE) * 2 + o % 2 == i).astype(F32).astype(BF16)

    b_up_high.wait_recv()
    b_down_low.wait_recv()
    b_up_low.wait_recv()
    b_down_high.wait_recv()
    embedded = chip_sum(3) + b_in[0].astype(F32) + b_in[1].astype(F32)
    e_keep[...] = embedded
    e_rows = embedded.astype(BF16)

    def scatter_plane(k, src, dst, ssem, rsem, sign):
        @pl.loop(0 if k else 1, GROUP)
        def _(d):
            to = (g + near(d)) % GROUP
            remote(
                src.at[k, pl.ds(pl.multiple_of(to * PIECE, PIECE), PIECE)],
                dst.at[k, pl.ds(pl.multiple_of(g * PIECE, PIECE), PIECE)],
                ssem.at[k], rsem.at[k], in_plane(sign * k, to),
            ).start()

        if k == 0:
            mine = pl.ds(pl.multiple_of(g * PIECE, PIECE), PIECE)
            dst[0, mine, :] = src[0, mine, :]

    def pieces(k, src, dst, ssem, rsem):
        n = CHUNK if k else CHUNK - PIECE
        return remote(
            src.at[k, pl.ds(0, n)], dst.at[k, pl.ds(0, n)], ssem.at[k], rsem.at[k], sibling
        )

    def scatter_z(k, src, dst, ssem, rsem, sign):
        @pl.loop(0, Z - 1)
        def _(t):
            d = far_first(t)
            rows = pl.ds(pl.multiple_of(d * TILE, TILE), TILE)
            remote(
                src.at[k, rows], dst.at[k, rows], ssem.at[k], rsem.at[k], along_z(sign * d)
            ).start()

        dst[k, :TILE, :] = src[k, :TILE, :]

    def tiles(k, src, dst, ssem, rsem):
        n = CHUNK - TILE
        return remote(
            src.at[k, pl.ds(0, n)], dst.at[k, pl.ds(0, n)], ssem.at[k], rsem.at[k], sibling
        )

    for k in OUT_ORDER:
        p1[k] = dot(hot[k * CHUNK : (k + 1) * CHUNK, :], e_rows).astype(BF16)
        scatter_plane(k, p1, r1, s1_s, s1_r, 1)

    w1_group.wait_recv()
    w1_rows = jnp.concatenate(
        [w1_in[k] for k in range(GROUP)] + [jnp.zeros((120, 128), F32)], axis=0
    ).astype(BF16)
    w2_all = jnp.zeros((64, 128), F32)
    for r in range(2):
        pick = (iota((64, 128), 0) * 2 + r == iota((64, 128), 1)).astype(F32).astype(BF16)
        put = (iota((128, 128), 0) * 2 + r == iota((128, 128), 1) % TILE).astype(F32).astype(BF16)
        w2_all += dot(dot_nt(pick, w1_rows).astype(BF16), put)
    w2_all = jnp.where(iota((64, 128), 0) // Z == iota((64, 128), 1) // TILE, w2_all, 0.0)
    for k in range(64):
        w2[k // Z, k % Z] = w2_all[k : k + 1]
    for k in range(Z):
        wx[0, k] = w2[0, k]
    for k in range(1, X):
        sent.append(
            remote(w2.at[k], wx.at[k], wx_s.at[k], wx_r.at[k], (((x + k) % X) * Z + z, g))
        )
        sent[-1].start()
    wx_copies = sent[-3:]

    def widths_along_z():
        for copy in wx_copies:
            copy.wait_recv()
        for k in range(Z):
            wz[k] = wx[0, k] + wx[1, k] + wx[2, k] + wx[3, k]
        w2_in[0] = wz[0]

        @pl.loop(0, Z - 1)
        def _(t):
            d = far_first(t)
            remote(wz.at[d], w2_in.at[d], w2_s, w2_r, (x * Z + (z + d) % Z, g)).start()

    w2_group = remote(wz.at[pl.ds(0, Z - 1)], w2_in.at[pl.ds(0, Z - 1)], w2_s, w2_r, sibling)
    sent.append(w2_group)

    for k in OUT_ORDER:
        arrived = pieces(k, p1, r1, s1_s, s1_r)
        arrived.wait_recv()
        sent.append(arrived)
        p2[k] = dot(perm, r1[k]).astype(BF16)
        if k == OUT_ORDER[2]:
            widths_along_z()
        scatter_z(k, p2, emb, s2_s, s2_r, 1)

    slot_col = as_columns(slot.astype(F32)).astype(I32)
    for m in range(8):
        hot_t[:, m * 128 : (m + 1) * 128] = (
            (slot_col == iota((ROWS, 128), 1) + m * 128).astype(F32).astype(BF16)
        )
    perm_t[...] = (((i // 2) % 8) * PIECE + (i // TILE) * 2 + i % 2 == o).astype(F32).astype(BF16)
    live_col = as_columns(live.astype(F32)) == 1.0
    e_keep[...] = jnp.where(live_col, 0.25, 1.0) * e_keep[...]

    w2_group.wait_recv()
    w2_rows = jnp.concatenate(
        [w2_in[k] for k in range(Z)] + [jnp.zeros((128 - Z, 128), F32)], axis=0
    ).astype(BF16)
    s, lane = iota((SLOTS, 128), 0), iota((SLOTS, 128), 1)
    spread = dot((s // TILE % Z == lane).astype(F32).astype(BF16), w2_rows)
    own = jnp.where(s // CHUNK * TILE + s % TILE == lane, spread, 0.0).astype(BF16)
    w_col = dot(own, jnp.ones((128, 128), BF16))
    rw = jnp.where(w_col > 0, 1.0 / jnp.where(w_col > 0, w_col, 1.0), 0.0)
    rw_col[...] = rw
    rw_row[...] = as_row(rw)

    begun = set()
    for n, k in enumerate(OUT_ORDER):
        arrived = tiles(k, p2, emb, s2_s, s2_r)
        arrived.wait_recv()
        sent.append(arrived)
        part = slice(k * CHUNK, (k + 1) * CHUNK)
        wide = emb[k].astype(F32)
        norm = jnp.broadcast_to(jnp.sum(wide * wide, axis=1, keepdims=True), (CHUNK, 128))
        norm_col[k] = norm
        norm_row[:, part] = as_row(norm)
        ones[k] = jnp.concatenate(
            [emb[k], (rw_col[part, :] > 0).astype(F32).astype(BF16)], axis=1
        )
        seen = OUT_ORDER[: n + 1]
        for a, b in [(k, m) for m in seen] + [(m, k) for m in seen[:-1]]:
            at_a, at_b = slice(a * CHUNK, (a + 1) * CHUNK), slice(b * CHUNK, (b + 1) * CHUNK)
            distance = (
                norm_col[a][:, 0:1] + norm_row[:, at_b] - 2.0 * dot_nt(emb[a], emb[b])
            )
            affinity = jnp.exp(-distance * rw_col[at_a, 0:1] * rw_row[:, at_b]).astype(BF16)
            aff[a, :, at_b] = affinity
            moved = dot(affinity, ones[b])
            both[a] = both[a] + moved if a in begun else moved
            begun.add(a)
    for k in range(4):
        part = slice(k * CHUNK, (k + 1) * CHUNK)
        here = rw_col[part, :] > 0
        inverse = jnp.where(here, 1.0 / jnp.where(here, both[k, :, COMPS:], 1.0), 0.0)
        moved = both[k, :, :COMPS] * inverse
        o_keep[k] = 0.25 * moved
        rw_col[part, :] = 0.5 * inverse
        s1_ref[part, :] = jnp.where(here, 0.5 * (emb[k].astype(F32) + moved), 0.0).astype(BF16)

    for k in BACK_ORDER:
        part = slice(k * CHUNK, (k + 1) * CHUNK)
        p3[k] = (o_keep[k] + rw_col[part, :] * dot(aff[k], s1_ref[...])).astype(BF16)
        scatter_z(k, p3, rz, s3_s, s3_r, -1)

    for k in BACK_ORDER:
        arrived = tiles(k, p3, rz, s3_s, s3_r)
        arrived.wait_recv()
        sent.append(arrived)
        p4[k] = dot(perm_t[...], rz[k]).astype(BF16)
        scatter_plane(k, p4, r4, s4_s, s4_r, -1)

    total = e_keep[...]
    for k in BACK_ORDER:
        arrived = pieces(k, p4, r4, s4_s, s4_r)
        arrived.wait_recv()
        sent.append(arrived)
        total += dot(hot_t[:, k * CHUNK : (k + 1) * CHUNK], r4[k])
    out_ref[...] = total

    finish()


def body(expression, loading, kernel_width, cluster, quality):
    hbm = pl.BlockSpec(memory_space=pltpu.HBM)
    vmem = pl.BlockSpec(memory_space=pltpu.VMEM)
    dma = pltpu.SemaphoreType.DMA
    chunks = pltpu.VMEM((4, CHUNK, COMPS), BF16)
    operands = [
        pltpu.with_memory_space_constraint(a, pltpu.HBM)
        for a in (
            expression,
            loading,
            kernel_width,
            cluster.reshape(1, ROWS),
            quality.reshape(1, ROWS),
        )
    ]
    return pl.pallas_call(
        kernel,
        out_shape=jax.ShapeDtypeStruct((ROWS, COMPS), F32),
        in_specs=[hbm] * 5,
        out_specs=vmem,
        scratch_shapes=[
            pltpu.VMEM((8, ROWS, 512), BF16),
            pltpu.VMEM((4, ROWS, COMPS), F32),
            pltpu.VMEM((CHUNK, CHUNK), BF16),
            pltpu.VMEM((512, COMPS), BF16),
            pltpu.VMEM((ROWS,), BF16),
            pltpu.VMEM((1, ROWS), I32),
            pltpu.VMEM((1, ROWS), I32),
            pltpu.VMEM((4, ROWS, COMPS), BF16),
            pltpu.VMEM((4, ROWS, COMPS), BF16),
            pltpu.VMEM((ROWS, COMPS), BF16),
            pltpu.VMEM((2, HALF, COMPS), BF16),
            pltpu.VMEM((2, ROWS, COMPS), BF16),
            pltpu.VMEM((2, ROWS, COMPS), BF16),
            pltpu.VMEM((2, HALF, COMPS), F32),
            pltpu.VMEM((ROWS, COMPS), F32),
            pltpu.VMEM((SLOTS, ROWS), BF16),
            pltpu.VMEM((ROWS, SLOTS), BF16),
            chunks,
            chunks,
            chunks,
            chunks,
            pltpu.VMEM((GROUP, 1, 128), F32),
            pltpu.VMEM((GROUP, 1, 128), F32),
            pltpu.VMEM((X, Z, 1, 128), F32),
            pltpu.VMEM((X, Z, 1, 128), F32),
            pltpu.VMEM((Z, 1, 128), F32),
            pltpu.VMEM((Z, 1, 128), F32),
            pltpu.VMEM((SLOTS, 128), F32),
            pltpu.VMEM((1, SLOTS), F32),
            pltpu.VMEM((4, CHUNK, SLOTS), BF16),
            pltpu.VMEM((4, CHUNK, 128), F32),
            pltpu.VMEM((1, SLOTS), F32),
            pltpu.VMEM((4, CHUNK, 2 * COMPS), BF16),
            pltpu.VMEM((4, CHUNK, 2 * COMPS), F32),
            pltpu.VMEM((4, CHUNK, COMPS), F32),
            pltpu.VMEM((SLOTS, COMPS), BF16),
            chunks,
            chunks,
            chunks,
            chunks,
            dma((8,)), dma((4,)), dma((4,)), dma((4,)), dma((2,)), dma((2,)), dma((4,)), dma((4,)),
            dma((4,)), dma((4,)), dma((4,)), dma((4,)), dma((4,)), dma((4,)), dma((4,)), dma((4,)),
            dma, dma, dma((4,)), dma((4,)), dma, dma,
        ],
        compiler_params=pltpu.CompilerParams(
            collective_id=0, has_side_effects=True, vmem_limit_bytes=48 * 1024 * 1024
        ),
    )(*operands)


def solution(mesh):
    return jax.shard_map(
        body,
        mesh=mesh,
        in_specs=(
            P("cells", "genes"),
            P("genes", None),
            P(("cells", "genes")),
            P(("cells", "genes"), None),
            P(("cells", "genes")),
        ),
        out_specs=P(("cells", "genes"), None),
        check_vma=False,
    )
```

time: 70.9 us -> 68.6 us (0.968)
  Pallas kernels: 70.1 us -> 67.8 us
    pallas_call x1, Pallas kernels: 70.1 us -> 67.8 us  [body(): pl.pallas_call(kernel, out_shape=jax.ShapeDtypeStruct((ROWS, COMPS), F32)...]
where the time goes in v3:
time: 68.6 us; the launch traced here: 68.5 us
  Pallas kernels  67.8 us (99%)
  local copies, waits for them, and re-layouts  0.71 us (1%)
    pallas_call x1, Pallas kernels, body(): pl.pallas_call(kernel, out_shape=jax.ShapeDtypeStruct((ROWS, COMPS), F32)...  67.8 us

profile of v3, /device:TPU:1, one launch (start us, length us, event | category | flops | bytes accessed | tf_op | source)
XLA Modules:
  0.0 68.5 jit_solution(13977494938375889811)
XLA Ops:
  0.0 67.8 %shard_map.55 = f32[512,128]{1,0:T(8,128)S(1)} custom-call(bf16[4096,512]{1,0:T(8,128)(2,1)} %expr.1, bf16[512,128]{1,0:T(8,128)(2,1)} %load_hbm.1, bf16[512]{0:T(512)(128)(2,1)} %width_hbm.1, s32[1,512]{1,0:T(1,128)} %bitcast.2, s32[1,512]{1,0:T(1,128)} %bitcast.3), custom_call_target="tpu_custom_call" | custom-call | tf_op jit(solution)/shard_map/pallas_call | solution.py:431
  67.8 0.7 %copy.7 = f32[512,128]{1,0:T(8,128)} copy(f32[512,128]{1,0:T(8,128)S(1)} %shard_map.55) | data formatting | bytes 524288

commit v4 on v3

--- a/solution.py
+++ b/solution.py
@@ -395,6 +395,9 @@
         p3[k] = (o_keep[k] + rw_col[part, :] * dot(aff[k], s1_ref[...])).astype(BF16)
         scatter_z(k, p3, rz, s3_s, s3_r, -1)
 
+    finish()
+    sent.clear()
+
     for k in BACK_ORDER:
         arrived = tiles(k, p3, rz, s3_s, s3_r)
         arrived.wait_recv()

time: 68.6 us -> 68.6 us (level)
  no operation moved by 1% of the time
where the time goes in v4:
time: 68.6 us; the launch traced here: 68.5 us
  Pallas kernels  67.8 us (99%)
  local copies, waits for them, and re-layouts  0.71 us (1%)
    pallas_call x1, Pallas kernels, body(): pl.pallas_call(kernel, out_shape=jax.ShapeDtypeStruct((ROWS, COMPS), F32)...  67.8 us

profile of v4, /device:TPU:1, one launch (start us, length us, event | category | flops | bytes accessed | tf_op | source)
XLA Modules:
  0.0 68.5 jit_solution(5316673270686092529)
XLA Ops:
  0.0 67.8 %shard_map.55 = f32[512,128]{1,0:T(8,128)S(1)} custom-call(bf16[4096,512]{1,0:T(8,128)(2,1)} %expr.1, bf16[512,128]{1,0:T(8,128)(2,1)} %load_hbm.1, bf16[512]{0:T(512)(128)(2,1)} %width_hbm.1, s32[1,512]{1,0:T(1,128)} %bitcast.2, s32[1,512]{1,0:T(1,128)} %bitcast.3), custom_call_target="tpu_custom_call" | custom-call | tf_op jit(solution)/shard_map/pallas_call | solution.py:434
  67.8 0.7 %copy.7 = f32[512,128]{1,0:T(8,128)} copy(f32[512,128]{1,0:T(8,128)S(1)} %shard_map.55) | data formatting | bytes 524288
